TPU v7x, 256 devices: a whole 4x4x8 slice. The times are simulated.
256 devices in a mesh: dp: 32 (over z, y), mp: 8 (over x, core).
Axes of the slice: x: 4, y: 4, z: 8, core: 2. Of those that a mesh axis runs over, the one named last changes fastest.
Arguments:
- loaded: bfloat16 [5, 8192, 8192], P(None, ('dp', 'mp')), may hold values from -6 to 6
- row_plan: int32 [8192], P(('dp', 'mp')), may hold values from 0 to 8191, as said below
- lengths: int32 [3], replicated, may hold values from 1 to 4096, 8192 in all
- se_filter: bfloat16 [7, 512], P(None, 'mp'), may hold values from -2 to 2
- mr_filter: bfloat16 [128, 512], P(None, 'mp'), may hold values from -0.5 to 0.5
- grad_out: bfloat16 [8192, 8192], P('dp', 'mp'), may hold values from -6 to 6
Outputs:
- grad_loaded: bfloat16 [5, 8192, 8192], P(None, ('dp', 'mp'))
- se_grad: float32 [7, 512], P(None, 'mp')
- mr_grad: float32 [128, 512], P(None, 'mp')
Inputs may be any that keep to these rules, and one draw needn't show every extreme that they name: row_plan is a permutation of the 8192 packed rows; of the 256 loaded rows of one dp index at most 16 go to the packed rows k * 256 to (k + 1) * 256 - 1 of any one k, and exactly 16 to some k.
All inputs are finite; a program needn't handle non-finite values.
Results may differ from a plain program's by a relative error of at most 0.0075.
Values may be sent and summed in bfloat16 or wider, within the bound.
No kernel may reach another device: no remote copies, remote signals or barrier semaphores. Data moves between devices by JAX's collectives and lax.ppermute only.
A program may use at most 128 MiB of HBM per device.

v0:
```python
import jax
import jax.numpy as jnp
from jax import lax
from jax.sharding import PartitionSpec as P


def shifted(shard, axis, by):
    length = lax.axis_size(axis)
    pairs = [(i, i + by) for i in range(length) if 0 <= i + by < length]
    return lax.ppermute(shard, axis, pairs)


def sequence_starts(row_ids, lengths):
    finish = jnp.cumsum(lengths)
    passed = finish[None, :] <= row_ids[:, None]
    return jnp.sum(jnp.where(passed, lengths[None, :], 0), axis=1)


def band_tiles(taps_by_group, causal):
    tap_count, group_count = taps_by_group.shape
    columns = jnp.transpose(taps_by_group)
    if causal:
        head_row = jnp.concatenate(
            [
                jnp.zeros((group_count, 1), taps_by_group.dtype),
                columns[:, ::-1],
                jnp.zeros((group_count, tap_count), taps_by_group.dtype),
            ],
            axis=1,
        )
    else:
        head_row = jnp.concatenate(
            [columns, jnp.zeros((group_count, tap_count + 1), taps_by_group.dtype)], axis=1
        )
    repeated = jnp.tile(head_row, (1, tap_count))
    return repeated[:, : 2 * tap_count * tap_count].reshape(group_count, tap_count, 2 * tap_count)


def lag_sums(blocks):
    group_count, tap_count, span_width = blocks.shape
    flat_rows = blocks.reshape(group_count, tap_count * span_width)
    flat_rows = jnp.concatenate(
        [flat_rows, jnp.zeros((group_count, tap_count), blocks.dtype)], axis=1
    )
    skewed = flat_rows.reshape(group_count, tap_count, span_width + 1)
    return jnp.transpose(jnp.sum(skewed[:, :, 1 : tap_count + 1], axis=1)[:, ::-1])


def short_forward(padded, weights, starts, anchor, margin):
    out_rows = padded.shape[0] - margin
    targets = anchor + jnp.arange(out_rows, dtype=jnp.int32)
    result = jnp.zeros((out_rows, padded.shape[1]), jnp.float32)
    for step_lag in range(weights.shape[0]):
        source = padded[margin - step_lag : margin - step_lag + out_rows].astype(jnp.float32)
        allowed = (targets - step_lag >= starts)[:, None]
        result = result + jnp.where(allowed, source * weights[step_lag][None, :], 0.0)
    return result


def short_backward(extended, weights, later_starts, anchor, out_rows):
    sources = anchor + jnp.arange(out_rows, dtype=jnp.int32)
    result = jnp.zeros((out_rows, extended.shape[1]), jnp.float32)
    for step_lag in range(weights.shape[0]):
        later = extended[step_lag : step_lag + out_rows].astype(jnp.float32)
        allowed = (sources >= later_starts[step_lag : step_lag + out_rows])[:, None]
        result = result + jnp.where(allowed, later * weights[step_lag][None, :], 0.0)
    return result


def short_grads(grad_rows, padded, starts, anchor, margin, tap_count, group_count):
    out_rows = grad_rows.shape[0]
    channels = grad_rows.shape[1]
    targets = anchor + jnp.arange(out_rows, dtype=jnp.int32)
    outcome = []
    for step_lag in range(tap_count):
        source = padded[margin - step_lag : margin - step_lag + out_rows].astype(jnp.float32)
        allowed = (targets - step_lag >= starts)[:, None]
        terms = jnp.where(allowed, grad_rows.astype(jnp.float32) * source, 0.0)
        outcome.append(
            jnp.sum(terms.reshape(out_rows, group_count, channels // group_count), axis=(0, 2))
        )
    return jnp.stack(outcome)


def long_forward(extended, tiles, starts, anchor):
    group_count, tap_count, span_width = tiles.shape
    channels = extended.shape[1]
    per_group = channels // group_count
    slab_count = (extended.shape[0] - tap_count) // tap_count

    def one_slab(slab_index):
        slab_start = slab_index * tap_count
        window = lax.dynamic_slice_in_dim(extended, slab_start, span_width, 0).reshape(
            span_width, group_count, per_group
        )
        row_starts = lax.dynamic_slice_in_dim(starts, slab_start, tap_count, 0)
        sources = anchor + slab_start - tap_count + jnp.arange(span_width, dtype=jnp.int32)
        keep_mask = (sources[None, :] >= row_starts[:, None]).astype(tiles.dtype)
        mixed_rows = jnp.einsum(
            "gim,mgc->igc",
            tiles * keep_mask[None, :, :],
            window,
            preferred_element_type=jnp.float32,
        )
        return mixed_rows.reshape(tap_count, channels)

    return lax.map(one_slab, jnp.arange(slab_count, dtype=jnp.int32)).reshape(
        slab_count * tap_count, channels
    )


def long_backward(extended, tiles, later_starts, anchor):
    group_count, tap_count, span_width = tiles.shape
    channels = extended.shape[1]
    per_group = channels // group_count
    slab_count = (extended.shape[0] - tap_count) // tap_count

    def one_slab(slab_index):
        slab_start = slab_index * tap_count
        window = lax.dynamic_slice_in_dim(extended, slab_start, span_width, 0).reshape(
            span_width, group_count, per_group
        )
        their_starts = lax.dynamic_slice_in_dim(later_starts, slab_start, span_width, 0)
        sources = anchor + slab_start + jnp.arange(tap_count, dtype=jnp.int32)
        keep_mask = (sources[:, None] >= their_starts[None, :]).astype(tiles.dtype)
        mixed_rows = jnp.einsum(
            "gim,mgc->igc",
            tiles * keep_mask[None, :, :],
            window,
            preferred_element_type=jnp.float32,
        )
        return mixed_rows.reshape(tap_count, channels)

    return lax.map(one_slab, jnp.arange(slab_count, dtype=jnp.int32)).reshape(
        slab_count * tap_count, channels
    )


def long_grads(grad_rows, extended, starts, anchor, tap_count, group_count):
    channels = grad_rows.shape[1]
    per_group = channels // group_count
    span_width = 2 * tap_count
    slab_count = grad_rows.shape[0] // tap_count

    def one_slab(carry, slab_index):
        slab_start = slab_index * tap_count
        window = lax.dynamic_slice_in_dim(extended, slab_start, span_width, 0).reshape(
            span_width, group_count, per_group
        )
        rows_here = lax.dynamic_slice_in_dim(grad_rows, slab_start, tap_count, 0).reshape(
            tap_count, group_count, per_group
        )
        row_starts = lax.dynamic_slice_in_dim(starts, slab_start, tap_count, 0)
        sources = anchor + slab_start - tap_count + jnp.arange(span_width, dtype=jnp.int32)
        keep_mask = (sources[None, :] >= row_starts[:, None]).astype(jnp.float32)
        grid = jnp.einsum("igc,mgc->gim", rows_here, window, preferred_element_type=jnp.float32)
        return (carry + grid * keep_mask[None, :, :], None)

    initial = jnp.zeros((group_count, tap_count, span_width), jnp.float32)
    summed, unused = lax.scan(one_slab, initial, jnp.arange(slab_count, dtype=jnp.int32))
    return lag_sums(summed)


def on_device(loaded, row_plan, lengths, se_filter, mr_filter, grad_out):
    shards = lax.axis_size("dp")
    dp_index = lax.axis_index("dp")
    local_rows = grad_out.shape[0]
    channels = grad_out.shape[1]
    group_count = se_filter.shape[1]
    per_group = channels // group_count
    tap_count = mr_filter.shape[0]
    short_taps = se_filter.shape[0]
    margin = 8
    capacity = 2 * local_rows // shards
    anchor = dp_index * local_rows
    full_plan = lax.all_gather(row_plan, ("dp", "mp"), axis=0, tiled=True)
    group_plan = lax.dynamic_slice_in_dim(full_plan, anchor, local_rows, 0)
    target = group_plan // local_rows
    matches = (target[:, None] == jnp.arange(shards, dtype=jnp.int32)[None, :]).astype(jnp.int32)
    earlier = jnp.cumsum(matches, axis=0) - matches
    packed_at = target * capacity + jnp.sum(earlier * matches, axis=1)
    every_plan = full_plan.reshape(shards, local_rows)
    arriving = (every_plan // local_rows == dp_index).astype(jnp.int32)
    arrival_rank = jnp.cumsum(arriving, axis=1) - arriving
    sent_from = jnp.arange(shards, dtype=jnp.int32)[:, None] * capacity + arrival_rank
    landing = jnp.where(arriving == 1, every_plan % local_rows, local_rows)
    source_of = (
        jnp.zeros((local_rows,), jnp.int32)
        .at[landing.reshape(-1)]
        .set(sent_from.reshape(-1), mode="drop")
    )
    columns = lax.all_to_all(loaded, "mp", split_axis=2, concat_axis=1, tiled=True)
    parcels = (
        jnp.zeros((columns.shape[0], shards * capacity, channels), jnp.bfloat16)
        .at[:, packed_at, :]
        .set(columns)
    )
    received = lax.all_to_all(parcels, "dp", split_axis=1, concat_axis=1, tiled=True)
    context = received[:, source_of, :]
    gate_one = context[0]
    key_one = context[1]
    value_one = context[2]
    gate_two = context[3]
    key_two = context[4]
    inner_one = (key_one.astype(jnp.float32) * value_one.astype(jnp.float32)).astype(jnp.bfloat16)
    here_rows = anchor + jnp.arange(local_rows, dtype=jnp.int32)
    starts_here = sequence_starts(here_rows, lengths)
    later_rows = anchor + jnp.arange(local_rows + tap_count, dtype=jnp.int32)
    later_starts = sequence_starts(later_rows, lengths)
    short_weights = jnp.repeat(se_filter.astype(jnp.float32), per_group, axis=1)
    forward_tiles = band_tiles(mr_filter, True)
    backward_tiles = band_tiles(mr_filter, False)
    inner_rim = shifted(inner_one[local_rows - margin :], "dp", 1)
    padded_one = jnp.concatenate([inner_rim, inner_one], axis=0)
    short_mix = short_forward(padded_one, short_weights, starts_here, anchor, margin)
    middle = (gate_one.astype(jnp.float32) * short_mix).astype(jnp.bfloat16)
    inner_two = (key_two.astype(jnp.float32) * middle.astype(jnp.float32)).astype(jnp.bfloat16)
    inner_rim_two = shifted(inner_two[local_rows - tap_count :], "dp", 1)
    padded_two = jnp.concatenate([inner_rim_two, inner_two], axis=0)
    long_mix = long_forward(padded_two, forward_tiles, starts_here, anchor)
    cotangent = grad_out.astype(jnp.float32)
    grad_mix_two = (cotangent * gate_two.astype(jnp.float32)).astype(jnp.bfloat16)
    grad_gate_two = (cotangent * long_mix).astype(jnp.bfloat16)
    back_rim = shifted(grad_mix_two[:tap_count], "dp", -1)
    grad_inner_two = long_backward(
        jnp.concatenate([grad_mix_two, back_rim], axis=0), backward_tiles, later_starts, anchor
    )
    grad_key_two = (grad_inner_two * middle.astype(jnp.float32)).astype(jnp.bfloat16)
    grad_middle = grad_inner_two * key_two.astype(jnp.float32)
    grad_gate_one = (grad_middle * short_mix).astype(jnp.bfloat16)
    grad_mix_one = (grad_middle * gate_one.astype(jnp.float32)).astype(jnp.bfloat16)
    short_back = shifted(grad_mix_one[:margin], "dp", -1)
    grad_inner_one = short_backward(
        jnp.concatenate([grad_mix_one, short_back], axis=0),
        short_weights,
        later_starts[: local_rows + margin],
        anchor,
        local_rows,
    ).astype(jnp.bfloat16)
    long_part = long_grads(grad_mix_two, padded_two, starts_here, anchor, tap_count, group_count)
    short_part = short_grads(
        grad_mix_one, padded_one, starts_here, anchor, margin, short_taps, group_count
    )
    short_total, long_total = lax.psum((short_part, long_part), "dp")
    unit_scale = (local_rows * shards * per_group) ** (-0.5)
    grad_key_one = (grad_inner_one.astype(jnp.float32) * value_one.astype(jnp.float32)).astype(
        jnp.bfloat16
    )
    grad_value_one = (grad_inner_one.astype(jnp.float32) * key_one.astype(jnp.float32)).astype(
        jnp.bfloat16
    )
    returning = jnp.stack(
        [grad_gate_one, grad_key_one, grad_value_one, grad_gate_two, grad_key_two]
    )
    outbound = (
        jnp.zeros((returning.shape[0], shards * capacity, channels), jnp.bfloat16)
        .at[:, source_of, :]
        .set(returning)
    )
    returned = lax.all_to_all(outbound, "dp", split_axis=1, concat_axis=1, tiled=True)
    own_rows = returned[:, packed_at, :]
    restored = lax.all_to_all(own_rows, "mp", split_axis=1, concat_axis=2, tiled=True)
    return (restored, short_total * unit_scale, long_total * unit_scale)


def solution(mesh):
    placed = (
        P(None, ("dp", "mp"), None),
        P(("dp", "mp")),
        P(),
        P(None, "mp"),
        P(None, "mp"),
        P("dp", "mp"),
    )
    return jax.shard_map(
        on_device,
        mesh=mesh,
        in_specs=placed,
        out_specs=(P(None, ("dp", "mp"), None), P(None, "mp"), P(None, "mp")),
        check_vma=False,
    )
```

profile of v0, /device:TPU:4, one launch (start us, length us, event | category | flops | bytes accessed | tf_op | source)
XLA Modules:
  0.0 939.2 jit_solution(16717614205049255059)
XLA Ops:
  0.6 14.7 %copy.86 = bf16[5,32,8192]{1,0,2:T(8,128)(2,1)} copy(bf16[5,32,8192]{2,1,0:T(8,128)(2,1)} %param.12) | data formatting | bytes 5242880 | tf_op args[0]
  15.4 13.7 %reshape.441 = bf16[8,2,81920]{2,1,0:T(2,128)(2,1)} reshape(bf16[8192,5,32]{2,1,0:T(8,128)(2,1)} %bitcast.199) | data formatting | bytes 5242880
  29.1 5.9 all-to-all-start
  35.3 99.3 %all-reduce.2 = s32[8192]{0:T(1024)S(1)} all-reduce(s32[8192]{0:T(1024)S(1)} %dynamic-update-slice), channel_id=1, replica_groups=mesh['dp'=32,'mp'=8] {'dp','mp'}, use_global_device_ids=true, to_apply=%add.2 | all-reduce | flops 8192 | bytes 65536
  135.8 11.8 %reshape.442 = bf16[8192,5,32]{2,1,0:T(8,128)(2,1)} reshape(bf16[8,2,81920]{2,1,0:T(2,128)(2,1)S(1)} %all-to-all-done) | data formatting | bytes 5242880
  147.7 19.8 %copy.87 = bf16[5,8,32,1024]{3,0,2,1:T(8,128)(2,1)} copy(bf16[5,8,32,1024]{2,0,3,1:T(8,128)(2,1)} %bitcast.198) | data formatting | bytes 5242880 | tf_op jit(solution)/shard_map/all_to_all | solution.py:192
  167.4 4.3 broadcast.301.clone
  171.7 33.6 %scatter_fusion = bf16[5,512,1024]{2,0,1:T(8,128)(2,1)} fusion(bf16[5,512,1024]{2,0,1:T(8,128)(2,1)} %broadcast.301.clone, s32[256]{0:T(256)S(1)} %compare_select_fusion.1, bf16[256,5,1024]{2,1,0:T(8,128)(2,1)} %bitcast.211), kind=kCustom, calls=%fused_computation.3 | custom fusion | bytes 7865344 | tf_op jit(solution)/shard_map/scatter | solution.py:196
  205.3 6.6 all-to-all-start.1
  213.3 3.2 tile.8
  216.5 10.8 %tile.9 = bf16[64,32896]{1,0:T(8,128)(2,1)} reshape(bf16[64,128,257]{2,1,0:T(8,128)(2,1)} %tile.8) | data formatting | bytes 8421376 | tf_op jit(solution)/shard_map/tile | solution.py:35
  229.5 3.0 copy.130
  233.9 3.2 tile.20
  237.1 10.8 %tile.21 = bf16[64,32896]{1,0:T(8,128)(2,1)} reshape(bf16[64,128,257]{2,1,0:T(8,128)(2,1)} %tile.20) | data formatting | bytes 8421376 | tf_op jit(solution)/shard_map/tile | solution.py:35
  250.1 3.0 copy.131
  253.1 30.4 %scatter_custom_fusion = s32[256]{0:T(256)S(1)} fusion(s32[8192]{0:T(1024)S(1)} %get-tuple-element.414, s32[8192]{0:T(1024)S(1)} %get-tuple-element.413, s32[]{:T(128)} %copy.203), kind=kCustom, calls=%fused_computation.206 | custom fusion | bytes 1028 | tf_op jit(solution)/shard_map/scatter | solution.py:190
  285.1 117.5 %all-to-all-done.1 = bf16[5,512,1024]{2,0,1:T(8,128)(2,1)} async-done(((bf16[5,512,1024]{2,0,1:T(8,128)(2,1)}), bf16[5,512,1024]{2,0,1:T(8,128)(2,1)}, u32[]{:S(2)}, u32[]{:S(2)}) %all-to-all-start.1) | async-done | bytes 5242912 | tf_op jit(solution)/shard_map/all_to_all | solution.py:198
  402.5 6.2 gather_fusion
  408.7 14.2 %slice_convert_fusion.1 = (f32[1,256,1024]{2,0,1:T(1,128)S(1)}, bf16[1,256,1024]{2,0,1:T(2,128)(2,1)S(1)}, bf16[1,256,1024]{2,0,1:T(2,128)(2,1)S(1)}, f32[1,256,1024]{2,0,1:T(1,128)S(1)}, bf16[1,256,1024]{2,0,1:T(2,128)(2,1)}) fusion(bf16[5,256,1024]{2,0,1:T(8,128)(2,1)} %bitcast.207), kind=kLoop, calls=%fused_computation.93 | loop fusion | flops 524288 | bytes 6291456 | tf_op jit(solution)/shard_map/convert_element_type | solution.py:205
  425.0 4.7 collective-permute-start.1
  433.0 13.2 %while.38 = (s32[]{:T(128)}, f32[2,128,1024]{1,2,0:T(8,128)}, s32[2]{0:T(128)}, bf16[384,1024]{1,0:T(8,128)(2,1)S(1)}, s32[]{:T(128)}, /*index=5*/s32[384]{0:T(512)S(1)}, bf16[64,128,256]{2,1,0:T(8,128)(2,1)}, s32[1]{0:T(128)}) while((s32[]{:T(128)}, f32[2,128,1024]{1,2,0:T(8,128)}, s32[2]{0:T(128)}, ...), condition=%wide.region_10.11_spmd.clone, body=%wide.region_9.10_spmd.sunk.clone | while | flops 69271688 | bytes 8524455 | solution.py:134
  435.4 3.4 fusion.106
  442.0 3.4 fusion.106
  447.9 5.9 fusion.23
  459.4 5.6 collective-permute-done.2
  465.0 2.8 fusion.52
  470.1 11.9 %while.39 = (s32[]{:T(128)}, f32[2,128,1024]{2,1,0:T(8,128)}, s32[2]{0:T(128)S(1)}, bf16[384,1024]{0,1:T(8,128)(2,1)S(1)}, s32[]{:T(128)}, /*index=5*/s32[256]{0:T(256)S(1)}, bf16[64,128,256]{2,1,0:T(8,128)(2,1)}, s32[1]{0:T(128)}) while((s32[]{:T(128)}, f32[2,128,1024]{2,1,0:T(8,128)}, s32[2]{0:T(128)S(1)}, ...), condition=%wide.region_13.14_spmd.clone, body=%wide.region_12.13_spmd.sunk.clone | while | flops 69271816 | bytes 8523980 | solution.py:107
  471.6 3.4 fusion.109
  477.5 3.4 fusion.109
  486.2 5.3 copy.95
  491.4 4.3 broadcast.301
  495.7 33.5 %scatter_fusion.1 = bf16[5,512,1024]{2,0,1:T(8,128)(2,1)} fusion(bf16[5,512,1024]{2,0,1:T(8,128)(2,1)} %broadcast.301, s32[256]{0:T(256)S(1)} %compare_select_fusion.2, bf16[256,5,1024]{2,1,0:T(8,128)(2,1)} %copy.95), kind=kCustom, calls=%fused_computation.4 | custom fusion | bytes 7865344 | tf_op jit(solution)/shard_map/scatter | solution.py:258
  529.2 15.3 %all-to-all-start.2 = ((bf16[5,512,1024]{2,0,1:T(8,128)(2,1)}), bf16[5,512,1024]{2,0,1:T(8,128)(2,1)}, u32[]{:S(2)}, u32[]{:S(2)}) async-start(bf16[5,512,1024]{2,0,1:T(8,128)(2,1)} %scatter_fusion.1), calls=%async_computation.2 | async-start | bytes 16777216 | tf_op jit(solution)/shard_map/all_to_all | solution.py:260
  549.6 5.6 convert_convert_fusion
  556.4 2.6 copy.99
  562.2 161.6 %all-to-all-done.2 = bf16[5,512,1024]{2,0,1:T(8,128)(2,1)} async-done(((bf16[5,512,1024]{2,0,1:T(8,128)(2,1)}), bf16[5,512,1024]{2,0,1:T(8,128)(2,1)}, u32[]{:S(2)}, u32[]{:S(2)}) %all-to-all-start.2) | async-done | bytes 5242912 | tf_op jit(solution)/shard_map/all_to_all | solution.py:260
  723.8 6.2 gather_fusion.1
  730.0 11.7 %all-to-all-start.3 = ((bf16[5,256,1024]{2,0,1:T(8,128)(2,1)}), bf16[5,256,1024]{2,0,1:T(8,128)(2,1)}, u32[]{:S(2)}, u32[]{:S(2)}) async-start(bf16[5,256,1024]{2,0,1:T(8,128)(2,1)} %bitcast.212), calls=%async_computation.3 | async-start | bytes 8388608 | tf_op jit(solution)/shard_map/all_to_all | solution.py:262
  741.7 16.0 %while.40 = (s32[]{:T(128)}, f32[64,128,256]{2,1,0:T(8,128)}, s32[2]{0:T(128)S(1)}, bf16[256,1024]{1,0:T(8,128)(2,1)S(1)}, bf16[384,1024]{0,1:T(8,128)(2,1)S(1)}, /*index=5*/s32[]{:T(128)}, s32[256]{0:T(256)S(1)}, s32[1]{0:T(128)}) while((s32[]{:T(128)}, f32[64,128,256]{2,1,0:T(8,128)}, s32[2]{0:T(128)S(1)}, ...), condition=%wide.region_31.32_spmd.clone.clone, body=%wide.region_30.31_spmd.clone.sunk.clone | while | flops 73466120 | bytes 19926744 | solution.py:160
  743.4 4.6 select_add_fusion.3
  749.7 8.0 select_add_fusion.3
  757.7 8.1 copy.132
  765.8 3.8 concatenate.27
  769.5 14.1 %reshape.378 = f32[64,128,257]{2,1,0:T(8,128)} reshape(f32[64,32896]{1,0:T(8,128)} %concatenate.27) | data formatting | bytes 16842752 | tf_op jit(solution)/shard_map/reshape | solution.py:45
  783.7 4.5 slice_reduce_fusion
  788.3 142.4 %all-reduce.3 = (f32[7,64]{1,0:T(8,128)S(1)}, f32[128,64]{0,1:T(8,128)S(1)}) all-reduce(f32[7,64]{1,0:T(8,128)S(1)} %stack.55, f32[128,64]{0,1:T(8,128)S(1)} %bitcast.220), channel_id=1, replica_groups=mesh['dp'=32,'mp'=8] {'dp'}, use_global_device_ids=true, to_apply=%region_29.30 | all-reduce | flops 8640 | bytes 69120 | tf_op jit(solution)/shard_map/psum | solution.py:244
  932.0 3.9 copy.96
  935.9 3.1 all_to_all.41
  (206 shorter events, 50.1 us)
Async XLA Ops:
  29.1 5.9 copy-start.25
  29.1 106.7 %all-to-all-start = ((bf16[8,2,81920]{2,1,0:T(2,128)(2,1)}), bf16[8,2,81920]{2,1,0:T(2,128)(2,1)S(1)}, u32[]{:S(2)}, u32[]{:S(2)}) async-start(bf16[8,2,81920]{2,1,0:T(2,128)(2,1)} %reshape.441), calls=%async_computation | async-start | bytes 5242880 | tf_op jit(solution)/shard_map/all_to_all | solution.py:192
  205.3 7.7 copy-start.24
  205.3 7.9 copy-start.10
  205.3 197.2 %all-to-all-start.1 = ((bf16[5,512,1024]{2,0,1:T(8,128)(2,1)}), bf16[5,512,1024]{2,0,1:T(8,128)(2,1)}, u32[]{:S(2)}, u32[]{:S(2)}) async-start(bf16[5,512,1024]{2,0,1:T(8,128)(2,1)} %scatter_fusion), calls=%async_computation.1 | async-start | bytes 16777216 | tf_op jit(solution)/shard_map/all_to_all | solution.py:198
  227.3 2.2 slice-start
  229.5 3.0 copy-start.23
  247.9 2.2 slice-start.1
  408.7 14.2 %copy-start.9 = (bf16[256,1024]{1,0:T(8,128)(2,1)S(1)}, bf16[256,1024]{1,0:T(8,128)(2,1)}, u32[]{:S(2)}) copy-start(bf16[256,1024]{1,0:T(8,128)(2,1)} %param.17) | copy-start | bytes 1572868
  422.9 6.9 copy-start.2
  422.9 9.5 %copy-start.4 = (f32[1,256,1024]{2,0,1:T(1,128)}, f32[1,256,1024]{2,0,1:T(1,128)S(1)}, u32[]{:S(2)}) copy-start(f32[1,256,1024]{2,0,1:T(1,128)S(1)} %get-tuple-element.409) | copy-start | bytes 3145732
  423.2 9.2 collective-permute-start
  425.0 7.4 copy-start.6
  425.0 22.8 %collective-permute-start.1 = (bf16[8,1024]{1,0:T(8,128)(2,1)S(1)}, bf16[8,1024]{1,0:T(8,128)(2,1)S(1)}, u32[]{:S(2)}, u32[]{:S(2)}) collective-permute-start(bf16[8,1024]{1,0:T(8,128)(2,1)S(1)} %slice.236), channel_id=1, source_target_pairs={{0,8},{8,16},{16,24},{24,32},{32,40},{40,48},{48,56},{56,64},{64,7... | collective-permute-start | bytes 49160 | tf_op jit(solution)/shard_map/ppermute | solution.py:10
  447.8 8.1 copy-start
  447.8 8.1 copy-start.7
  447.8 8.1 copy-start.11
  447.8 8.1 copy-start.12
  447.8 8.1 copy-start.13
  447.8 8.1 copy-start.14
  447.9 8.1 copy-start.15
  454.2 10.8 %copy-start.5 = (f32[1,256,1024]{2,0,1:T(1,128)S(1)}, f32[1,256,1024]{2,0,1:T(1,128)}, u32[]{:S(2)}) copy-start(f32[1,256,1024]{2,0,1:T(1,128)} %copy-done.4) | copy-start | bytes 3145732
  454.2 10.8 %copy-start.16 = (pred[256]{0:T(512)(128)(4,1)S(1)}, pred[256]{0:T(512)(128)(4,1)}, u32[]{:S(2)}) copy-start(pred[256]{0:T(512)(128)(4,1)} %get-tuple-element.422) | copy-start | bytes 772
  454.2 10.8 %copy-start.17 = (pred[256]{0:T(512)(128)(4,1)S(1)}, pred[256]{0:T(512)(128)(4,1)}, u32[]{:S(2)}) copy-start(pred[256]{0:T(512)(128)(4,1)} %get-tuple-element.423) | copy-start | bytes 772
  454.2 10.8 %copy-start.18 = (pred[256]{0:T(512)(128)(4,1)S(1)}, pred[256]{0:T(512)(128)(4,1)}, u32[]{:S(2)}) copy-start(pred[256]{0:T(512)(128)(4,1)} %get-tuple-element.424) | copy-start | bytes 772
  454.3 10.8 %copy-start.19 = (pred[256]{0:T(512)(128)(4,1)S(1)}, pred[256]{0:T(512)(128)(4,1)}, u32[]{:S(2)}) copy-start(pred[256]{0:T(512)(128)(4,1)} %get-tuple-element.425) | copy-start | bytes 772
  454.3 10.8 %copy-start.20 = (pred[256]{0:T(512)(128)(4,1)S(1)}, pred[256]{0:T(512)(128)(4,1)}, u32[]{:S(2)}) copy-start(pred[256]{0:T(512)(128)(4,1)} %get-tuple-element.426) | copy-start | bytes 772
  454.3 10.8 %copy-start.21 = (pred[256]{0:T(512)(128)(4,1)S(1)}, pred[256]{0:T(512)(128)(4,1)}, u32[]{:S(2)}) copy-start(pred[256]{0:T(512)(128)(4,1)} %get-tuple-element.427) | copy-start | bytes 772
  454.3 10.8 %copy-start.22 = (pred[256]{0:T(512)(128)(4,1)S(1)}, pred[256]{0:T(512)(128)(4,1)}, u32[]{:S(2)}) copy-start(pred[256]{0:T(512)(128)(4,1)} %get-tuple-element.428) | copy-start | bytes 772
  454.3 13.6 %copy-start.3 = (f32[1,256,1024]{2,0,1:T(1,128)S(1)}, f32[1,256,1024]{2,0,1:T(1,128)}, u32[]{:S(2)}) copy-start(f32[1,256,1024]{2,0,1:T(1,128)} %copy-done.2) | copy-start | bytes 3145732
  454.3 13.9 %collective-permute-start.3 = (bf16[128,1024]{1,0:T(8,128)(2,1)S(1)}, bf16[128,1024]{1,0:T(8,128)(2,1)S(1)}, u32[]{:S(2)}, u32[]{:S(2)}) collective-permute-start(bf16[128,1024]{1,0:T(8,128)(2,1)S(1)} %slice.259), channel_id=1, source_target_pairs={{0,8},{8,16},{16,24},{24,32},{32,40},{40,48},{48,56},{56,64},{64,7... | collective-permute-start | bytes 786440 | tf_op jit(solution)/shard_map/ppermute | solution.py:10
  458.0 7.0 collective-permute-start.2
  468.2 1.5 copy-start.8
  529.2 15.3 %copy-start.1 = (bf16[1,256,1024]{2,0,1:T(2,128)(2,1)S(1)}, bf16[1,256,1024]{2,0,1:T(2,128)(2,1)}, u32[]{:S(2)}) copy-start(bf16[1,256,1024]{2,0,1:T(2,128)(2,1)} %get-tuple-element.410) | copy-start | bytes 1572868
  529.2 194.6 %all-to-all-start.2 = ((bf16[5,512,1024]{2,0,1:T(8,128)(2,1)}), bf16[5,512,1024]{2,0,1:T(8,128)(2,1)}, u32[]{:S(2)}, u32[]{:S(2)}) async-start(bf16[5,512,1024]{2,0,1:T(8,128)(2,1)} %scatter_fusion.1), calls=%async_computation.2 | async-start | bytes 16777216 | tf_op jit(solution)/shard_map/all_to_all | solution.py:260
  730.0 202.0 %all-to-all-start.3 = ((bf16[5,256,1024]{2,0,1:T(8,128)(2,1)}), bf16[5,256,1024]{2,0,1:T(8,128)(2,1)}, u32[]{:S(2)}, u32[]{:S(2)}) async-start(bf16[5,256,1024]{2,0,1:T(8,128)(2,1)} %bitcast.212), calls=%async_computation.3 | async-start | bytes 8388608 | tf_op jit(solution)/shard_map/all_to_all | solution.py:262
where the time goes:
time: 948 us; the launch traced here: 939 us
  waiting for transfers between devices  287 us (30%)
  local copies, waits for them, and re-layouts  281 us (30%)
  blocking collectives  242 us (26%)
  other arithmetic  48.8 us (5%)
  starting transfers between devices  48.4 us (5%)
  matrix products  26.1 us (3%)
    all_to_all x1, waiting for transfers between devices, on_device(): lax.all_to_all(outbound, 'dp', split_axis=1, concat_axis=1, tiled=True)  162 us
    psum x1, blocking collectives, on_device(): short_total, long_total = lax.psum((short_part, long_part), 'dp')  142 us
    all_to_all x1, waiting for transfers between devices, on_device(): lax.all_to_all(parcels, 'dp', split_axis=1, concat_axis=1, tiled=True)  117 us
    unnamed x1, blocking collectives  99.3 us
    unnamed x63, local copies, waits for them, and re-layouts  57.5 us
    scatter x1, local copies, waits for them, and re-layouts, on_device(): parcels = jnp.zeros((columns.shape[0], shards * capacity, channels), jnp....  33.6 us
    scatter x1, local copies, waits for them, and re-layouts, on_device(): outbound = jnp.zeros((returning.shape[0], shards * capacity, channels), j...  33.5 us
    scatter x1, local copies, waits for them, and re-layouts, on_device(): source_of = jnp.zeros((local_rows,), jnp.int32).at[landing.reshape(-1)].s...  30.4 us
  transfers between devices with their start and end apart: 8, of which 4 were waited for; matrix products, arithmetic and copies ran while one was open for 16% of the time, Pallas kernels for 0%

commit v1 on v0

--- a/solution.py
+++ b/solution.py
@@ -2,6 +2,29 @@
 import jax.numpy as jnp
 from jax import lax
 from jax.sharding import PartitionSpec as P
+
+
+def in_blocks(value, dim, peers):
+    before, after = (value.shape[:dim], value.shape[dim + 1 :])
+    return jnp.moveaxis(value.reshape(*before, peers, -1, *after), dim, 0)
+
+
+def laid_out(blocks, dim):
+    shape = list(blocks.shape[1:])
+    shape[dim] *= blocks.shape[0]
+    return jnp.moveaxis(blocks, 0, dim).reshape(shape)
+
+
+def exchange_directly(x, axis, split_dim, concat_dim):
+    length, index = (lax.axis_size(axis), lax.axis_index(axis))
+    blocks = in_blocks(x, split_dim, length)
+    out = blocks
+    for turn in range(1, length):
+        target, source = ((index + turn) % length, (index - turn) % length)
+        sent = lax.dynamic_index_in_dim(blocks, target, 0)
+        theirs = lax.ppermute(sent, axis, [(i, (i + turn) % length) for i in range(length)])
+        out = lax.dynamic_update_slice_in_dim(out, theirs, source, axis=0)
+    return laid_out(out, concat_dim)
 
 
 def shifted(shard, axis, by):
@@ -259,7 +282,7 @@
     )
     returned = lax.all_to_all(outbound, "dp", split_axis=1, concat_axis=1, tiled=True)
     own_rows = returned[:, packed_at, :]
-    restored = lax.all_to_all(own_rows, "mp", split_axis=1, concat_axis=2, tiled=True)
+    restored = exchange_directly(own_rows, "mp", 1, 2)
     return (restored, short_total * unit_scale, long_total * unit_scale)
 
 

time: 948 us -> 941 us (level); the launches traced: 939 us -> 922 us
  waiting for transfers between devices: 287 us -> 139 us
  blocking collectives: 242 us -> 345 us
  starting transfers between devices: 48.4 us -> 74.2 us
    all_to_all x1, waiting for transfers between devices: 162 us -> 0.01 us  [on_device(): lax.all_to_all(outbound, 'dp', split_axis=1, concat_axis=1, tiled=True)]
    psum x1, blocking collectives: 142 us -> 246 us  [on_device(): short_total, long_total = lax.psum((short_part, long_part), 'dp')]
    ppermute x0 -> x7, starting transfers between devices: none -> 37.2 us  [exchange_directly(): lax.ppermute(sent, axis, [(i, (i + turn) % length) for i in range(length)])]
    ppermute x0 -> x7, waiting for transfers between devices: none -> 13.7 us  [exchange_directly(): lax.ppermute(sent, axis, [(i, (i + turn) % length) for i in range(length)])]
    all_to_all x1 -> x0, starting transfers between devices: 11.7 us -> none  [on_device(): lax.all_to_all(own_rows, 'mp', split_axis=1, concat_axis=2, tiled=True)]
    unnamed x63 -> x65, local copies, waits for them, and re-layouts: 57.5 us -> 57.7 us
  transfers between devices with their start and end apart: 8 -> 14, of which waited for: 4 -> 6; matrix products, arithmetic and copies ran while one was open for 16% -> 17% of each run, Pallas kernels for 0% -> 0%
where the time goes in v1:
time: 941 us; the launch traced here: 922 us
  blocking collectives  345 us (37%)
  local copies, waits for them, and re-layouts  283 us (30%)
  waiting for transfers between devices  139 us (15%)
  starting transfers between devices  74.2 us (8%)
  other arithmetic  48.9 us (5%)
  matrix products  26.1 us (3%)
    psum x1, blocking collectives, on_device(): short_total, long_total = lax.psum((short_part, long_part), 'dp')  246 us
    all_to_all x1, waiting for transfers between devices, on_device(): lax.all_to_all(parcels, 'dp', split_axis=1, concat_axis=1, tiled=True)  117 us
    unnamed x1, blocking collectives  99.3 us
    unnamed x65, local copies, waits for them, and re-layouts  57.7 us
    ppermute x7, starting transfers between devices, exchange_directly(): lax.ppermute(sent, axis, [(i, (i + turn) % length) for i in range(length)])  37.2 us
    scatter x1, local copies, waits for them, and re-layouts, on_device(): parcels = jnp.zeros((columns.shape[0], shards * capacity, channels), jnp....  33.6 us
    scatter x1, local copies, waits for them, and re-layouts, on_device(): outbound = jnp.zeros((returning.shape[0], shards * capacity, channels), j...  33.5 us
    scatter x1, local copies, waits for them, and re-layouts, on_device(): source_of = jnp.zeros((local_rows,), jnp.int32).at[landing.reshape(-1)].s...  30.4 us
  transfers between devices with their start and end apart: 14, of which 6 were waited for; matrix products, arithmetic and copies ran while one was open for 17% of the time, Pallas kernels for 0%

profile of v1, /device:TPU:4, one launch (start us, length us, event | category | flops | bytes accessed | tf_op | source)
XLA Modules:
  0.0 922.5 jit_solution(11796817693514229520)
XLA Ops:
  0.6 14.7 %copy.86 = bf16[5,32,8192]{1,0,2:T(8,128)(2,1)} copy(bf16[5,32,8192]{2,1,0:T(8,128)(2,1)} %param.12) | data formatting | bytes 5242880 | tf_op args[0]
  15.4 13.7 %reshape.456 = bf16[8,2,81920]{2,1,0:T(2,128)(2,1)} reshape(bf16[8192,5,32]{2,1,0:T(8,128)(2,1)} %bitcast.215) | data formatting | bytes 5242880
  29.1 5.9 all-to-all-start
  35.3 99.3 %all-reduce.2 = s32[8192]{0:T(1024)S(1)} all-reduce(s32[8192]{0:T(1024)S(1)} %dynamic-update-slice), channel_id=1, replica_groups=mesh['dp'=32,'mp'=8] {'dp','mp'}, use_global_device_ids=true, to_apply=%add.2 | all-reduce | flops 8192 | bytes 65536
  135.8 11.8 %reshape.457 = bf16[8192,5,32]{2,1,0:T(8,128)(2,1)} reshape(bf16[8,2,81920]{2,1,0:T(2,128)(2,1)S(1)} %all-to-all-done) | data formatting | bytes 5242880
  147.7 19.8 %copy.87 = bf16[5,8,32,1024]{3,0,2,1:T(8,128)(2,1)} copy(bf16[5,8,32,1024]{2,0,3,1:T(8,128)(2,1)} %bitcast.214) | data formatting | bytes 5242880 | tf_op jit(solution)/shard_map/all_to_all | solution.py:215
  167.4 4.3 broadcast.315.clone
  171.7 33.6 %scatter_fusion = bf16[5,512,1024]{2,0,1:T(8,128)(2,1)} fusion(bf16[5,512,1024]{2,0,1:T(8,128)(2,1)} %broadcast.315.clone, s32[256]{0:T(256)S(1)} %compare_select_fusion.1, bf16[256,5,1024]{2,1,0:T(8,128)(2,1)} %bitcast.230), kind=kCustom, calls=%fused_computation.3 | custom fusion | bytes 7865344 | tf_op jit(solution)/shard_map/scatter | solution.py:219
  205.3 6.3 all-to-all-start.1
  213.0 3.2 tile.8
  216.2 10.8 %tile.9 = bf16[64,32896]{1,0:T(8,128)(2,1)} reshape(bf16[64,128,257]{2,1,0:T(8,128)(2,1)} %tile.8) | data formatting | bytes 8421376 | tf_op jit(solution)/shard_map/tile | solution.py:58
  229.2 3.2 copy.130
  233.7 3.2 tile.20
  236.9 10.8 %tile.21 = bf16[64,32896]{1,0:T(8,128)(2,1)} reshape(bf16[64,128,257]{2,1,0:T(8,128)(2,1)} %tile.20) | data formatting | bytes 8421376 | tf_op jit(solution)/shard_map/tile | solution.py:58
  249.9 3.0 copy.131
  253.0 30.4 %scatter_custom_fusion = s32[256]{0:T(256)S(1)} fusion(s32[8192]{0:T(1024)S(1)} %get-tuple-element.421, s32[8192]{0:T(1024)S(1)} %get-tuple-element.420, s32[]{:T(128)} %copy.210), kind=kCustom, calls=%fused_computation.220 | custom fusion | bytes 1028 | tf_op jit(solution)/shard_map/scatter | solution.py:213
  284.9 117.3 %all-to-all-done.1 = bf16[5,512,1024]{2,0,1:T(8,128)(2,1)} async-done(((bf16[5,512,1024]{2,0,1:T(8,128)(2,1)}), bf16[5,512,1024]{2,0,1:T(8,128)(2,1)}, u32[]{:S(2)}, u32[]{:S(2)}) %all-to-all-start.1) | async-done | bytes 5242912 | tf_op jit(solution)/shard_map/all_to_all | solution.py:221
  402.2 6.2 gather_fusion
  408.4 14.2 %slice_convert_fusion.1 = (f32[1,256,1024]{2,0,1:T(1,128)S(1)}, bf16[1,256,1024]{2,0,1:T(2,128)(2,1)S(1)}, bf16[1,256,1024]{2,0,1:T(2,128)(2,1)S(1)}, f32[1,256,1024]{2,0,1:T(1,128)S(1)}, bf16[1,256,1024]{2,0,1:T(2,128)(2,1)}) fusion(bf16[5,256,1024]{2,0,1:T(8,128)(2,1)} %bitcast.226), kind=kLoop, calls=%fused_computation.93 | loop fusion | flops 524288 | bytes 6291456 | tf_op jit(solution)/shard_map/convert_element_type | solution.py:228
  424.8 4.8 collective-permute-start.1
  432.8 13.4 %while.38 = (s32[]{:T(128)}, f32[2,128,1024]{1,2,0:T(8,128)}, s32[2]{0:T(128)}, bf16[384,1024]{1,0:T(8,128)(2,1)S(1)}, s32[]{:T(128)}, /*index=5*/s32[384]{0:T(512)S(1)}, bf16[64,128,256]{2,1,0:T(8,128)(2,1)}, s32[1]{0:T(128)}) while((s32[]{:T(128)}, f32[2,128,1024]{1,2,0:T(8,128)}, s32[2]{0:T(128)}, ...), condition=%wide.region_10.11_spmd.clone, body=%wide.region_9.10_spmd.sunk.clone | while | flops 69271688 | bytes 8524455 | solution.py:157
  435.3 3.4 fusion.106
  442.0 3.4 fusion.106
  447.9 5.9 fusion.23
  459.4 5.6 collective-permute-done.2
  470.1 11.9 %while.39 = (s32[]{:T(128)}, f32[2,128,1024]{2,1,0:T(8,128)}, s32[2]{0:T(128)S(1)}, bf16[384,1024]{0,1:T(8,128)(2,1)S(1)}, s32[]{:T(128)}, /*index=5*/s32[256]{0:T(256)S(1)}, bf16[64,128,256]{2,1,0:T(8,128)(2,1)}, s32[1]{0:T(128)}) while((s32[]{:T(128)}, f32[2,128,1024]{2,1,0:T(8,128)}, s32[2]{0:T(128)S(1)}, ...), condition=%wide.region_13.14_spmd.clone, body=%wide.region_12.13_spmd.sunk.clone | while | flops 69271816 | bytes 8523980 | solution.py:130
  471.6 3.4 fusion.109
  477.5 3.4 fusion.109
  486.2 5.3 copy.95
  491.4 4.4 broadcast.315
  495.8 33.5 %scatter_fusion.1 = bf16[5,512,1024]{2,0,1:T(8,128)(2,1)} fusion(bf16[5,512,1024]{2,0,1:T(8,128)(2,1)} %broadcast.315, s32[256]{0:T(256)S(1)} %compare_select_fusion.2, bf16[256,5,1024]{2,1,0:T(8,128)(2,1)} %copy.95), kind=kCustom, calls=%fused_computation.4 | custom fusion | bytes 7865344 | tf_op jit(solution)/shard_map/scatter | solution.py:281
  529.4 15.7 %all-to-all-start.2 = ((bf16[5,512,1024]{2,0,1:T(8,128)(2,1)}), bf16[5,512,1024]{2,0,1:T(8,128)(2,1)}, u32[]{:S(2)}, u32[]{:S(2)}) async-start(bf16[5,512,1024]{2,0,1:T(8,128)(2,1)} %scatter_fusion.1), calls=%async_computation.2 | async-start | bytes 16777216 | tf_op jit(solution)/shard_map/all_to_all | solution.py:283
  550.4 5.6 convert_convert_fusion
  563.0 16.0 %while.40 = (s32[]{:T(128)}, f32[64,128,256]{2,1,0:T(8,128)}, s32[2]{0:T(128)S(1)}, bf16[256,1024]{1,0:T(8,128)(2,1)S(1)}, bf16[384,1024]{0,1:T(8,128)(2,1)S(1)}, /*index=5*/s32[]{:T(128)}, s32[256]{0:T(256)S(1)}, s32[1]{0:T(128)}) while((s32[]{:T(128)}, f32[64,128,256]{2,1,0:T(8,128)}, s32[2]{0:T(128)S(1)}, ...), condition=%wide.region_31.32_spmd.clone.clone, body=%wide.region_30.31_spmd.clone.sunk.clone | while | flops 73466120 | bytes 19926744 | solution.py:183
  564.7 4.6 select_add_fusion.3
  571.0 8.0 select_add_fusion.3
  579.0 8.1 copy.132
  587.1 3.8 concatenate.27
  590.9 14.3 %reshape.393 = f32[64,128,257]{2,1,0:T(8,128)} reshape(f32[64,32896]{1,0:T(8,128)} %concatenate.27) | data formatting | bytes 16842752 | tf_op jit(solution)/shard_map/reshape | solution.py:68
  605.2 4.5 slice_reduce_fusion
  609.8 246.1 %all-reduce.3 = (f32[7,64]{1,0:T(8,128)S(1)}, f32[128,64]{0,1:T(8,128)S(1)}) all-reduce(f32[7,64]{1,0:T(8,128)S(1)} %stack.55, f32[128,64]{0,1:T(8,128)S(1)} %bitcast.238), channel_id=1, replica_groups=mesh['dp'=32,'mp'=8] {'dp'}, use_global_device_ids=true, to_apply=%region_29.30 | all-reduce | flops 8640 | bytes 69120 | tf_op jit(solution)/shard_map/psum | solution.py:267
  855.9 6.1 gather_fusion.1
  865.3 3.8 collective-permute-start.6
  869.7 2.9 collective-permute-start.8
  872.6 5.0 collective-permute-done.4
  880.1 30.5 %collective-permute-start.10 = (bf16[1,5,32,1024]{3,1,2,0:T(8,128)(2,1)S(1)}, bf16[1,5,32,1024]{3,1,2,0:T(8,128)(2,1)S(1)}, u32[]{:S(2)}, u32[]{:S(2)}) collective-permute-start(bf16[1,5,32,1024]{3,1,2,0:T(8,128)(2,1)S(1)} %get-tuple-element.406), channel_id=1, source_target_pairs={{0,7},{1,0},{2,1},{3,2},{4,3},{5,4},{6,5},{7,6},{8,15},{9,8},{10,9... | collective-permute-start | bytes 983048 | tf_op jit(solution)/shard_map/ppermute | solution.py:25
  911.1 6.3 collective-permute-done.10
  919.1 3.1 reshape.391
  (228 shorter events, 62.9 us)
Async XLA Ops:
  29.1 5.9 copy-start.26
  29.1 106.7 %all-to-all-start = ((bf16[8,2,81920]{2,1,0:T(2,128)(2,1)}), bf16[8,2,81920]{2,1,0:T(2,128)(2,1)S(1)}, u32[]{:S(2)}, u32[]{:S(2)}) async-start(bf16[8,2,81920]{2,1,0:T(2,128)(2,1)} %reshape.456), calls=%async_computation | async-start | bytes 5242880 | tf_op jit(solution)/shard_map/all_to_all | solution.py:215
  205.3 7.4 copy-start.25
  205.3 7.6 copy-start.11
  205.3 196.9 %all-to-all-start.1 = ((bf16[5,512,1024]{2,0,1:T(8,128)(2,1)}), bf16[5,512,1024]{2,0,1:T(8,128)(2,1)}, u32[]{:S(2)}, u32[]{:S(2)}) async-start(bf16[5,512,1024]{2,0,1:T(8,128)(2,1)} %scatter_fusion), calls=%async_computation.1 | async-start | bytes 16777216 | tf_op jit(solution)/shard_map/all_to_all | solution.py:221
  227.0 2.2 slice-start
  229.2 3.2 copy-start.24
  247.7 2.2 slice-start.1
  408.4 14.2 %copy-start.10 = (bf16[256,1024]{1,0:T(8,128)(2,1)S(1)}, bf16[256,1024]{1,0:T(8,128)(2,1)}, u32[]{:S(2)}) copy-start(bf16[256,1024]{1,0:T(8,128)(2,1)} %param.17) | copy-start | bytes 1572868
  422.6 6.9 copy-start.3
  422.6 9.5 %copy-start.5 = (f32[1,256,1024]{2,0,1:T(1,128)}, f32[1,256,1024]{2,0,1:T(1,128)S(1)}, u32[]{:S(2)}) copy-start(f32[1,256,1024]{2,0,1:T(1,128)S(1)} %get-tuple-element.416) | copy-start | bytes 3145732
  423.0 9.2 collective-permute-start
  424.8 7.4 copy-start.7
  424.8 23.0 %collective-permute-start.1 = (bf16[8,1024]{1,0:T(8,128)(2,1)S(1)}, bf16[8,1024]{1,0:T(8,128)(2,1)S(1)}, u32[]{:S(2)}, u32[]{:S(2)}) collective-permute-start(bf16[8,1024]{1,0:T(8,128)(2,1)S(1)} %slice.236), channel_id=1, source_target_pairs={{0,8},{8,16},{16,24},{24,32},{32,40},{40,48},{48,56},{56,64},{64,7... | collective-permute-start | bytes 49160 | tf_op jit(solution)/shard_map/ppermute | solution.py:33
  447.8 8.1 copy-start.1
  447.8 8.1 copy-start.8
  447.8 8.1 copy-start.12
  447.8 8.1 copy-start.13
  447.8 8.1 copy-start.14
  447.9 8.1 copy-start.15
  447.9 8.1 copy-start.16
  454.2 10.8 %copy-start.6 = (f32[1,256,1024]{2,0,1:T(1,128)S(1)}, f32[1,256,1024]{2,0,1:T(1,128)}, u32[]{:S(2)}) copy-start(f32[1,256,1024]{2,0,1:T(1,128)} %copy-done.5) | copy-start | bytes 3145732
  454.2 10.8 %copy-start.17 = (pred[256]{0:T(512)(128)(4,1)S(1)}, pred[256]{0:T(512)(128)(4,1)}, u32[]{:S(2)}) copy-start(pred[256]{0:T(512)(128)(4,1)} %get-tuple-element.429) | copy-start | bytes 772
  454.2 10.8 %copy-start.18 = (pred[256]{0:T(512)(128)(4,1)S(1)}, pred[256]{0:T(512)(128)(4,1)}, u32[]{:S(2)}) copy-start(pred[256]{0:T(512)(128)(4,1)} %get-tuple-element.430) | copy-start | bytes 772
  454.2 10.8 %copy-start.19 = (pred[256]{0:T(512)(128)(4,1)S(1)}, pred[256]{0:T(512)(128)(4,1)}, u32[]{:S(2)}) copy-start(pred[256]{0:T(512)(128)(4,1)} %get-tuple-element.431) | copy-start | bytes 772
  454.2 10.8 %copy-start.20 = (pred[256]{0:T(512)(128)(4,1)S(1)}, pred[256]{0:T(512)(128)(4,1)}, u32[]{:S(2)}) copy-start(pred[256]{0:T(512)(128)(4,1)} %get-tuple-element.432) | copy-start | bytes 772
  454.2 10.8 %copy-start.21 = (pred[256]{0:T(512)(128)(4,1)S(1)}, pred[256]{0:T(512)(128)(4,1)}, u32[]{:S(2)}) copy-start(pred[256]{0:T(512)(128)(4,1)} %get-tuple-element.433) | copy-start | bytes 772
  454.2 10.8 %copy-start.22 = (pred[256]{0:T(512)(128)(4,1)S(1)}, pred[256]{0:T(512)(128)(4,1)}, u32[]{:S(2)}) copy-start(pred[256]{0:T(512)(128)(4,1)} %get-tuple-element.434) | copy-start | bytes 772
  454.2 10.8 %copy-start.23 = (pred[256]{0:T(512)(128)(4,1)S(1)}, pred[256]{0:T(512)(128)(4,1)}, u32[]{:S(2)}) copy-start(pred[256]{0:T(512)(128)(4,1)} %get-tuple-element.435) | copy-start | bytes 772
  454.3 13.6 %copy-start.4 = (f32[1,256,1024]{2,0,1:T(1,128)S(1)}, f32[1,256,1024]{2,0,1:T(1,128)}, u32[]{:S(2)}) copy-start(f32[1,256,1024]{2,0,1:T(1,128)} %copy-done.3) | copy-start | bytes 3145732
  454.3 13.9 %collective-permute-start.3 = (bf16[128,1024]{1,0:T(8,128)(2,1)S(1)}, bf16[128,1024]{1,0:T(8,128)(2,1)S(1)}, u32[]{:S(2)}, u32[]{:S(2)}) collective-permute-start(bf16[128,1024]{1,0:T(8,128)(2,1)S(1)} %slice.259), channel_id=1, source_target_pairs={{0,8},{8,16},{16,24},{24,32},{32,40},{40,48},{48,56},{56,64},{64,7... | collective-permute-start | bytes 786440 | tf_op jit(solution)/shard_map/ppermute | solution.py:33
  457.9 7.0 collective-permute-start.2
  468.2 1.5 copy-start.9
  529.4 16.0 %copy-start.2 = (bf16[1,256,1024]{2,0,1:T(2,128)(2,1)S(1)}, bf16[1,256,1024]{2,0,1:T(2,128)(2,1)}, u32[]{:S(2)}) copy-start(bf16[1,256,1024]{2,0,1:T(2,128)(2,1)} %get-tuple-element.417) | copy-start | bytes 1572868
  529.4 326.6 %all-to-all-start.2 = ((bf16[5,512,1024]{2,0,1:T(8,128)(2,1)}), bf16[5,512,1024]{2,0,1:T(8,128)(2,1)}, u32[]{:S(2)}, u32[]{:S(2)}) async-start(bf16[5,512,1024]{2,0,1:T(8,128)(2,1)} %scatter_fusion.1), calls=%async_computation.2 | async-start | bytes 16777216 | tf_op jit(solution)/shard_map/all_to_all | solution.py:283
  862.1 15.6 %copy-start = (bf16[256,5,1024]{2,1,0:T(8,128)(2,1)S(1)}, bf16[256,5,1024]{2,1,0:T(8,128)(2,1)}, u32[]{:S(2)}) copy-start(bf16[256,5,1024]{2,1,0:T(8,128)(2,1)} %gather_fusion.1) | copy-start | bytes 7864324
  864.7 13.0 %collective-permute-start.4 = (bf16[1,5,32,1024]{3,1,2,0:T(8,128)(2,1)S(1)}, bf16[1,5,32,1024]{3,1,2,0:T(8,128)(2,1)S(1)}, u32[]{:S(2)}, u32[]{:S(2)}) collective-permute-start(bf16[1,5,32,1024]{3,1,2,0:T(8,128)(2,1)S(1)} %get-tuple-element.412), channel_id=1, source_target_pairs={{0,1},{1,2},{2,3},{3,4},{4,5},{5,6},{6,7},{7,0},{8,9},{9,10},{10,1... | collective-permute-start | bytes 983048 | tf_op jit(solution)/shard_map/ppermute | solution.py:25
  865.3 14.8 %collective-permute-start.5 = (bf16[1,5,32,1024]{3,1,2,0:T(8,128)(2,1)S(1)}, bf16[1,5,32,1024]{3,1,2,0:T(8,128)(2,1)S(1)}, u32[]{:S(2)}, u32[]{:S(2)}) collective-permute-start(bf16[1,5,32,1024]{3,1,2,0:T(8,128)(2,1)S(1)} %get-tuple-element.411), channel_id=1, source_target_pairs={{0,2},{1,3},{2,4},{3,5},{4,6},{5,7},{6,0},{7,1},{8,10},{9,11},{10,... | collective-permute-start | bytes 983048 | tf_op jit(solution)/shard_map/ppermute | solution.py:25
  865.3 45.4 %collective-permute-start.6 = (bf16[1,5,32,1024]{3,1,2,0:T(8,128)(2,1)S(1)}, bf16[1,5,32,1024]{3,1,2,0:T(8,128)(2,1)S(1)}, u32[]{:S(2)}, u32[]{:S(2)}) collective-permute-start(bf16[1,5,32,1024]{3,1,2,0:T(8,128)(2,1)S(1)} %get-tuple-element.410), channel_id=1, source_target_pairs={{0,3},{1,4},{2,5},{3,6},{4,7},{5,0},{6,1},{7,2},{8,11},{9,12},{10,... | collective-permute-start | bytes 983048 | tf_op jit(solution)/shard_map/ppermute | solution.py:25
  869.7 41.1 %collective-permute-start.7 = (bf16[1,5,32,1024]{3,1,2,0:T(8,128)(2,1)S(1)}, bf16[1,5,32,1024]{3,1,2,0:T(8,128)(2,1)S(1)}, u32[]{:S(2)}, u32[]{:S(2)}) collective-permute-start(bf16[1,5,32,1024]{3,1,2,0:T(8,128)(2,1)S(1)} %get-tuple-element.409), channel_id=1, source_target_pairs={{0,4},{1,5},{2,6},{3,7},{4,0},{5,1},{6,2},{7,3},{8,12},{9,13},{10,... | collective-permute-start | bytes 983048 | tf_op jit(solution)/shard_map/ppermute | solution.py:25
  869.7 41.2 %collective-permute-start.8 = (bf16[1,5,32,1024]{3,1,2,0:T(8,128)(2,1)S(1)}, bf16[1,5,32,1024]{3,1,2,0:T(8,128)(2,1)S(1)}, u32[]{:S(2)}, u32[]{:S(2)}) collective-permute-start(bf16[1,5,32,1024]{3,1,2,0:T(8,128)(2,1)S(1)} %get-tuple-element.408), channel_id=1, source_target_pairs={{0,5},{1,6},{2,7},{3,0},{4,1},{5,2},{6,3},{7,4},{8,13},{9,14},{10,... | collective-permute-start | bytes 983048 | tf_op jit(solution)/shard_map/ppermute | solution.py:25
  877.7 33.3 %collective-permute-start.9 = (bf16[1,5,32,1024]{3,1,2,0:T(8,128)(2,1)S(1)}, bf16[1,5,32,1024]{3,1,2,0:T(8,128)(2,1)S(1)}, u32[]{:S(2)}, u32[]{:S(2)}) collective-permute-start(bf16[1,5,32,1024]{3,1,2,0:T(8,128)(2,1)S(1)} %get-tuple-element.407), channel_id=1, source_target_pairs={{0,6},{1,7},{2,0},{3,1},{4,2},{5,3},{6,4},{7,5},{8,14},{9,15},{10,... | collective-permute-start | bytes 983048 | tf_op jit(solution)/shard_map/ppermute | solution.py:25
  880.1 37.2 %collective-permute-start.10 = (bf16[1,5,32,1024]{3,1,2,0:T(8,128)(2,1)S(1)}, bf16[1,5,32,1024]{3,1,2,0:T(8,128)(2,1)S(1)}, u32[]{:S(2)}, u32[]{:S(2)}) collective-permute-start(bf16[1,5,32,1024]{3,1,2,0:T(8,128)(2,1)S(1)} %get-tuple-element.406), channel_id=1, source_target_pairs={{0,7},{1,0},{2,1},{3,2},{4,3},{5,4},{6,5},{7,6},{8,15},{9,8},{10,9... | collective-permute-start | bytes 983048 | tf_op jit(solution)/shard_map/ppermute | solution.py:25
